TPU v7x, 32 devices: a whole 2x2x4 slice. The times are simulated.
32 devices in a mesh: blk: 4 (over y, x), expert: 8 (over z, core).
Axes of the slice: x: 2, y: 2, z: 4, core: 2. Of those that a mesh axis runs over, the one named last changes fastest.
Arguments:
- tokens: bfloat16 [8, 2048, 768], P('expert', 'blk'), may hold values from -6 to 6
- cotangent: bfloat16 [8, 2048, 768], P('expert', 'blk'), may hold values from -6 to 6
- loss_mask: int32 [8, 2048], P('expert', 'blk'), may hold values 0 or 1
- routes: int32 [8, 2048, 1], P('expert', 'blk'), may hold values from 0 to 7, as said below
- priority: int32 [8, 4, 512], P('expert', 'blk'), may hold values from 0 to 511, each once within a row
- histogram: int32 [8], replicated, may hold values from 0 to 999
- qkv_weight: bfloat16 [768, 2304], replicated, may hold values from -0.21875 to 0.21875
- proj_weight: bfloat16 [768, 768], replicated, may hold values from -5 to 5
- attn_gain: float32 [768], replicated, may hold values from 0.5 to 1.5
- moe_gain: float32 [768], replicated, may hold values from 0.5 to 1.5
- route_weight: float32 [768, 16], replicated, may hold values from -0.21875 to 0.21875
- anchor_table: float32 [8, 16], replicated, may hold values from -6 to 6
- first_weight: bfloat16 [8, 768, 3072], P('expert'), may hold values from -0.21875 to 0.21875
- second_weight: bfloat16 [8, 3072, 768], P('expert'), may hold values from -3.59375 to 3.59375
Outputs:
- block_out: bfloat16 [8, 2048, 768], P('expert', 'blk')
- grad_tokens: float32 [8, 2048, 768], P('expert', 'blk')
- grad_qkv: float32 [768, 2304], replicated
- grad_proj: float32 [768, 768], replicated
- grad_attn_gain: float32 [768], replicated
- grad_moe_gain: float32 [768], replicated
- grad_route: float32 [768, 16], replicated
- grad_anchor: float32 [8, 16], replicated
- grad_first: float32 [8, 768, 3072], P('expert', None, 'blk')
- grad_second: float32 [8, 3072, 768], P('expert', 'blk')
- histogram_out: int32 [8], replicated
Inputs may be any that keep to these rules, and one draw needn't show every extreme that they name: `priority`: within each block of 512 positions every value appears once. `routes`: every expert is named by some position.
All inputs are finite; a program needn't handle non-finite values. No bound on the sum of `loss_mask` on one device may be relied on, other than what follows from the above.
Results may differ from a plain program's by a relative error of at most 0.019.
Values may be sent and summed in bfloat16 or wider, within the bound.
A program may use at most 192 MiB of HBM per device.

v0:
```python
import jax
import jax.numpy as jnp
from jax import lax
from jax.sharding import PartitionSpec as P

HEADS = 12
HEAD_DIM = 64


TOP_PRECISION = lax.Precision.HIGHEST
EPSILON = 1e-05
ROUTER_SOFTNESS = 0.4
MASKED = -1e30


def layer_norm(values, norm_gain):
    average = jnp.mean(values, axis=-1, keepdims=True)
    centered = values - average
    variance = jnp.mean(centered * centered, axis=-1, keepdims=True)
    return centered * lax.rsqrt(variance + EPSILON) * norm_gain


def unit_rows(matrix):
    return matrix * lax.rsqrt(1.0 + jnp.sum(matrix * matrix, axis=-1, keepdims=True))


def router_gate(normalized_rows, route_matrix, anchors, route_onehot):
    projection_output = unit_rows(jnp.dot(normalized_rows, route_matrix, precision=TOP_PRECISION))
    expert_anchor_rows = unit_rows(anchors)
    route_logit_scores = (
        jnp.dot(projection_output, expert_anchor_rows.T, precision=TOP_PRECISION) / ROUTER_SOFTNESS
    )
    return jnp.sum(jax.nn.softmax(route_logit_scores, axis=-1) * route_onehot, axis=-1)


def masked_scores(queries, key_rows, query_first, key_first, score_scale):
    scores = (
        jnp.einsum("qhd,khd->hqk", queries, key_rows, preferred_element_type=jnp.float32)
        * score_scale
    )
    grid_shape = (queries.shape[0], key_rows.shape[0])
    query_place = query_first + lax.broadcasted_iota(jnp.int32, grid_shape, 0)
    key_place = key_first + lax.broadcasted_iota(jnp.int32, grid_shape, 1)
    return (scores, (key_place <= query_place)[None])


def over_blocks(step_fn, carried, arrays, block_rows):
    row_total = arrays[0].shape[0]
    block_count = row_total // block_rows
    stacked = tuple(
        (member.reshape((block_count, block_rows) + member.shape[1:]) for member in arrays)
    )

    def scan_step(running, packed):
        position, blocks = packed
        return (step_fn(running, blocks, position * block_rows), None)

    result, unused = lax.scan(
        scan_step, carried, (jnp.arange(block_count, dtype=jnp.int32), stacked)
    )
    return result


def body(
    tokens,
    cotangent,
    loss_mask,
    routes,
    priority,
    histogram,
    qkv_weight,
    proj_weight,
    attn_gain,
    moe_gain,
    route_weight,
    anchor_table,
    first_weight,
    second_weight,
):
    tok_rows = tokens.shape[1]
    model_width = tokens.shape[2]
    score_scale = HEAD_DIM ** (-0.5)
    query_first = lax.axis_index("blk") * tok_rows
    local_experts = first_weight.shape[0]
    experts_all = local_experts * lax.axis_size("expert")
    capacity = tok_rows // experts_all
    head_shape = (tok_rows, HEADS, HEAD_DIM)
    seq_rows = tok_rows * lax.axis_size("blk")
    route_ids = routes[0, :, 0]
    route_onehot = (
        route_ids[:, None] == lax.broadcasted_iota(jnp.int32, (tok_rows, experts_all), 1)
    ).astype(jnp.float32)
    count_rows = jnp.sum(route_onehot, axis=0)
    total_counts = lax.psum(count_rows.astype(jnp.int32), ("blk", "expert"))
    block_input = tokens[0].astype(jnp.float32)
    normed_attn, attn_norm_back = jax.vjp(layer_norm, block_input, attn_gain)
    normed_low = normed_attn.astype(jnp.bfloat16)
    query_key_value_mix = jnp.dot(
        normed_low, qkv_weight, preferred_element_type=jnp.float32
    ).astype(jnp.bfloat16)
    query_flat = query_key_value_mix[:, :model_width]
    queries = query_flat.reshape(head_shape)
    key_local = query_key_value_mix[:, model_width : 2 * model_width]
    value_local = query_key_value_mix[:, 2 * model_width :]

    def forward_step(carried, blocks, key_first):
        running_top, running_sum, running_out = carried
        key_rows = blocks[0].reshape(blocks[0].shape[0], HEADS, HEAD_DIM)
        value_rows = blocks[1].reshape(blocks[1].shape[0], HEADS, HEAD_DIM)
        scores, allowed = masked_scores(queries, key_rows, query_first, key_first, score_scale)
        top_new = jnp.maximum(running_top, jnp.max(jnp.where(allowed, scores, MASKED), axis=2))
        weights = jnp.where(allowed, jnp.exp(scores - top_new[:, :, None]), 0.0)
        factor = jnp.exp(running_top - top_new)
        running_sum = running_sum * factor + jnp.sum(weights, axis=2)
        running_out = running_out * factor.T[:, :, None] + jnp.einsum(
            "hqk,khd->qhd",
            weights.astype(jnp.bfloat16),
            value_rows,
            preferred_element_type=jnp.float32,
        )
        return (top_new, running_sum, running_out)

    initial = (
        jnp.full((HEADS, tok_rows), MASKED, jnp.float32),
        jnp.zeros((HEADS, tok_rows), jnp.float32),
        jnp.zeros(head_shape, jnp.float32),
    )
    running_top, running_sum, running_out = over_blocks(
        forward_step,
        initial,
        (
            lax.all_gather(key_local, "blk", axis=0, tiled=True),
            lax.all_gather(value_local, "blk", axis=0, tiled=True),
        ),
        tok_rows,
    )
    attention_result = running_out / running_sum.T[:, :, None]
    log_total = running_top + jnp.log(running_sum)
    attended_low = attention_result.reshape(tok_rows, model_width).astype(jnp.bfloat16)
    residual_stream = block_input + jnp.dot(
        attended_low, proj_weight, preferred_element_type=jnp.float32
    )
    normed_moe, moe_norm_back = jax.vjp(layer_norm, residual_stream, moe_gain)

    def gate_of(normalized_rows, route_matrix, anchors):
        return router_gate(normalized_rows, route_matrix, anchors, route_onehot)

    gate_value, gate_back = jax.vjp(gate_of, normed_moe, route_weight, anchor_table)
    order_rows = priority[0, 0]
    same_route = route_ids[:, None] == route_ids[None, :]
    earlier = order_rows[None, :] < order_rows[:, None]
    slot_ids = jnp.sum((same_route & earlier).astype(jnp.int32), axis=1)
    target = jnp.where(slot_ids < capacity, route_ids * capacity + slot_ids, -1)
    selector = lax.broadcasted_iota(jnp.int32, (tok_rows, tok_rows), 0) == target[None, :]
    selector_low = selector.astype(jnp.bfloat16)
    outgoing = jnp.dot(
        selector_low, normed_moe.astype(jnp.bfloat16), preferred_element_type=jnp.float32
    )
    outgoing = outgoing.astype(jnp.bfloat16).reshape(experts_all, capacity, model_width)
    arrived = lax.all_to_all(outgoing, "expert", split_axis=0, concat_axis=0, tiled=True)
    sources = arrived.shape[0] // local_experts
    grouped = arrived.reshape(sources, local_experts, arrived.shape[1], arrived.shape[2])
    hidden = jnp.einsum("secd,edf->secf", grouped, first_weight, preferred_element_type=jnp.float32)
    act_low = jax.nn.gelu(hidden).astype(jnp.bfloat16)
    result = jnp.einsum(
        "secf,efd->secd", act_low, second_weight, preferred_element_type=jnp.float32
    )
    result = result.astype(jnp.bfloat16).reshape(arrived.shape)
    returned = lax.all_to_all(result, "expert", split_axis=0, concat_axis=0, tiled=True)
    returned, arrived = (returned, arrived)
    fetched = jnp.einsum(
        "st,sd->td",
        selector_low,
        returned.reshape(tok_rows, model_width),
        preferred_element_type=jnp.float32,
    )
    block_out = (residual_stream + gate_value[:, None] * fetched).astype(jnp.bfloat16)[None]
    grad_out = cotangent[0].astype(jnp.float32) * loss_mask[0].astype(jnp.float32)[:, None]
    grad_fetched = grad_out * gate_value[:, None]
    grad_gate = jnp.sum(grad_out * fetched, axis=1)
    grad_slots = jnp.dot(selector.astype(jnp.float32), grad_fetched, precision=TOP_PRECISION)
    grad_slots = grad_slots.astype(jnp.bfloat16).reshape(experts_all, capacity, model_width)
    grad_arrived = lax.all_to_all(grad_slots, "expert", split_axis=0, concat_axis=0, tiled=True)
    sources = grad_arrived.shape[0] // local_experts
    slot_shape = (sources, local_experts, capacity, model_width)
    grouped_in = arrived.reshape(slot_shape)
    grouped_grad = grad_arrived.reshape(slot_shape)
    hidden = jnp.einsum(
        "secd,edf->secf", grouped_in, first_weight, preferred_element_type=jnp.float32
    )
    act_low = jax.nn.gelu(hidden).astype(jnp.bfloat16)
    grad_second = jnp.einsum(
        "secf,secd->efd", act_low, grouped_grad, preferred_element_type=jnp.float32
    )
    grad_act = jnp.einsum(
        "secd,efd->secf", grouped_grad, second_weight, preferred_element_type=jnp.float32
    )
    unused, gelu_back = jax.vjp(jax.nn.gelu, hidden)
    grad_hidden = gelu_back(grad_act)[0].astype(jnp.bfloat16)
    grad_first = jnp.einsum(
        "secd,secf->edf", grouped_in, grad_hidden, preferred_element_type=jnp.float32
    )
    grad_sent = jnp.einsum(
        "secf,edf->secd", grad_hidden, first_weight, preferred_element_type=jnp.float32
    )
    grad_sent = grad_sent.astype(jnp.bfloat16).reshape(grad_arrived.shape)
    grad_returned = lax.all_to_all(grad_sent, "expert", split_axis=0, concat_axis=0, tiled=True)
    grad_first, grad_second = (
        lax.psum_scatter(
            grad_first.astype(jnp.bfloat16), "blk", scatter_dimension=2, tiled=True
        ).astype(jnp.float32),
        lax.psum_scatter(
            grad_second.astype(jnp.bfloat16), "blk", scatter_dimension=1, tiled=True
        ).astype(jnp.float32),
    )
    grad_moe_rows = jnp.einsum(
        "st,sd->td",
        selector_low,
        grad_returned.reshape(tok_rows, model_width),
        preferred_element_type=jnp.float32,
    )
    grad_router_rows, grad_route, grad_anchor = gate_back(grad_gate)
    grad_residual_norm, grad_moe_gain = moe_norm_back(grad_moe_rows + grad_router_rows)
    grad_residual = grad_out + grad_residual_norm
    grad_attn_low = grad_residual.astype(jnp.bfloat16)
    grad_proj = jnp.dot(attended_low.T, grad_attn_low, preferred_element_type=jnp.float32)
    grad_attended_flat = jnp.dot(
        grad_attn_low, proj_weight.T, preferred_element_type=jnp.float32
    ).astype(jnp.bfloat16)
    grad_attended = grad_attended_flat.reshape(head_shape)
    delta_rows = jnp.sum(grad_attended.astype(jnp.float32) * attention_result, axis=2).T
    key_all, value_all = (
        lax.all_gather(key_local, "blk", axis=0, tiled=True),
        lax.all_gather(value_local, "blk", axis=0, tiled=True),
    )
    block_count = seq_rows // tok_rows
    key_blocks = key_all.reshape(block_count, tok_rows, model_width)
    value_blocks = value_all.reshape(block_count, tok_rows, model_width)

    def key_block_step(running_grad, packed):
        position, key_block, value_block = packed
        key_rows = key_block.reshape(head_shape)
        value_rows = value_block.reshape(head_shape)
        scores, allowed = masked_scores(
            queries, key_rows, query_first, position * tok_rows, score_scale
        )
        soft_rows = jnp.where(allowed, jnp.exp(scores - log_total[:, :, None]), 0.0)
        grad_values = jnp.einsum(
            "hqk,qhd->khd",
            soft_rows.astype(jnp.bfloat16),
            grad_attended,
            preferred_element_type=jnp.float32,
        )
        grad_soft = jnp.einsum(
            "qhd,khd->hqk", grad_attended, value_rows, preferred_element_type=jnp.float32
        )
        grad_scores = (soft_rows * (grad_soft - delta_rows[:, :, None])).astype(jnp.bfloat16)
        grad_keys = score_scale * jnp.einsum(
            "hqk,qhd->khd", grad_scores, queries, preferred_element_type=jnp.float32
        )
        running_grad = running_grad + score_scale * jnp.einsum(
            "hqk,khd->qhd", grad_scores, key_rows, preferred_element_type=jnp.float32
        )
        term = jnp.concatenate(
            [grad_keys.reshape(tok_rows, model_width), grad_values.reshape(tok_rows, model_width)],
            axis=1,
        )
        return (running_grad, term)

    grad_queries, stacked_terms = lax.scan(
        key_block_step,
        jnp.zeros(head_shape, jnp.float32),
        (jnp.arange(block_count, dtype=jnp.int32), key_blocks, value_blocks),
    )
    all_terms = stacked_terms.reshape(seq_rows, 2 * model_width)
    key_value_grads = lax.psum_scatter(
        all_terms.astype(jnp.bfloat16), "blk", scatter_dimension=0, tiled=True
    ).astype(jnp.float32)
    grad_query_rows = grad_queries.reshape(tok_rows, model_width)
    grad_qkv_rows = jnp.concatenate([grad_query_rows, key_value_grads], axis=1).astype(jnp.bfloat16)
    grad_qkv = jnp.dot(normed_low.T, grad_qkv_rows, preferred_element_type=jnp.float32)
    grad_normed = jnp.dot(grad_qkv_rows, qkv_weight.T, preferred_element_type=jnp.float32)
    grad_source_norm, grad_attn_gain = attn_norm_back(grad_normed)
    grad_tokens = (grad_residual + grad_source_norm)[None]
    grad_qkv, grad_proj, grad_attn_gain, grad_moe_gain, grad_route, grad_anchor = lax.psum(
        (grad_qkv, grad_proj, grad_attn_gain, grad_moe_gain, grad_route, grad_anchor),
        ("blk", "expert"),
    )
    histogram_out = histogram + total_counts
    return (
        block_out,
        grad_tokens,
        grad_qkv,
        grad_proj,
        grad_attn_gain,
        grad_moe_gain,
        grad_route,
        grad_anchor,
        grad_first,
        grad_second,
        histogram_out,
    )


def solution(mesh):
    in_specs = (
        P("expert", "blk", None),
        P("expert", "blk", None),
        P("expert", "blk"),
        P("expert", "blk", None),
        P("expert", "blk", None),
        P(),
        P(),
        P(),
        P(),
        P(),
        P(),
        P(),
        P("expert", None, None),
        P("expert", None, None),
    )
    out_specs = (
        P("expert", "blk", None),
        P("expert", "blk", None),
        P(),
        P(),
        P(),
        P(),
        P(),
        P(),
        P("expert", None, "blk"),
        P("expert", "blk", None),
        P(),
    )
    return jax.shard_map(body, mesh=mesh, in_specs=in_specs, out_specs=out_specs, check_vma=False)
```

profile of v0, /device:TPU:0, one launch (start us, length us, event | category | flops | bytes accessed | tf_op | source)
XLA Modules:
  0.0 865.7 jit_solution(4273704076640165361)
XLA Ops:
  18.5 42.8 %all-gather.5.cloned.1.call-done = bf16[2048,768]{1,0:T(8,128)(2,1)} async-done(((bf16[512,768]{1,0:T(8,128)(2,1)}), bf16[2048,768]{1,0:T(8,128)(2,1)}) %all-gather.5.cloned.1.call-update) | async-done | bytes 3145744 | tf_op jit(solution)/shard_map/all_gather | solution.py:133
  66.0 41.7 %all-gather.3.cloned.1.call-done = bf16[2048,768]{1,0:T(8,128)(2,1)} async-done(((bf16[512,768]{1,0:T(8,128)(2,1)}), bf16[2048,768]{1,0:T(8,128)(2,1)}) %all-gather.3.cloned.1.call-update) | async-done | bytes 3145744 | tf_op jit(solution)/shard_map/all_gather | solution.py:132
  112.4 63.6 %while.28 = (s32[]{:T(128)}, f32[12,512]{1,0:T(8,128)}, f32[12,512]{1,0:T(8,128)}, f32[512,12,64]{0,2,1:T(8,128)}, s32[4]{0:T(128)S(1)}, /*index=5*/s32[]{:T(128...) while((s32[]{:T(128)}, f32[12,512]{1,0:T(8,128)}, ...), condition=%wide.region_5.6_spmd.clone, body=%wide.region_2.5_spmd.clone.sunk | while | flops 841389056 | bytes 52338996 | solution.py:58
  188.3 19.7 %all-to-all-done = bf16[8,64,768]{2,1,0:T(8,128)(2,1)} async-done(((bf16[8,64,768]{2,1,0:T(8,128)(2,1)}), bf16[8,64,768]{2,1,0:T(8,128)(2,1)}, u32[]{:S(2)}, u32[]{:S(2)}) %all-to-all-start) | async-done | bytes 786464 | tf_op jit(solution)/shard_map/all_to_all | solution.py:160
  215.4 6.9 fusion.76
  233.7 13.8 %all-to-all-done.1 = bf16[8,64,768]{2,1,0:T(8,128)(2,1)} async-done(((bf16[8,64,768]{2,1,0:T(8,128)(2,1)}), bf16[8,64,768]{2,1,0:T(8,128)(2,1)}, u32[]{:S(2)}, u32[]{:S(2)}) %all-to-all-start.1) | async-done | bytes 786464 | tf_op jit(solution)/shard_map/all_to_all | solution.py:169
  255.4 23.6 %all_to_all.20 = bf16[8,64,768]{2,1,0:T(8,128)(2,1)S(1)} all-to-all(bf16[8,64,768]{2,1,0:T(8,128)(2,1)S(1)} %bitcast.303), channel_id=1, replica_groups=mesh['blk'=4,'expert'=8] {'expert'}, dimensions={0} | all-to-all | bytes 1572864 | tf_op jit(solution)/shard_map/all_to_all | solution.py:183
  278.9 8.2 fusion.27
  301.0 16.5 %all-to-all-done.3 = bf16[8,64,768]{2,1,0:T(8,128)(2,1)} async-done(((bf16[8,64,768]{2,1,0:T(8,128)(2,1)}), bf16[8,64,768]{2,1,0:T(8,128)(2,1)}, u32[]{:S(2)}, u32[]{:S(2)}) %all-to-all-start.3) | async-done | bytes 786464 | tf_op jit(solution)/shard_map/all_to_all | solution.py:207
  333.2 129.5 %while.29 = (s32[]{:T(128)}, f32[512,12,64]{0,2,1:T(8,128)}, bf16[4,512,1536]{2,1,0:T(8,128)(2,1)}, bf16[4,512,768]{1,2,0:T(8,128)(2,1)}, s32[4]{0:T(128)S(1)}, ...) while((s32[]{:T(128)}, f32[512,12,64]{0,2,1:T(8,128)}, ...), condition=%wide.region_21.22_spmd.clone, body=%wide.region_20.21_spmd.clone.sunk | while | flops 2050098176 | bytes 99369320 | solution.py:270
  349.0 7.1 fusion.217
  381.3 7.1 fusion.217
  413.7 7.1 fusion.217
  433.5 6.3 fusion.216
  446.0 7.1 fusion.217
  462.8 6.9 fusion.40
  470.1 8.5 fusion.41
  487.2 43.8 %reduce-scatter.4.cloned.1.call-done = bf16[512,1536]{1,0:T(8,128)(2,1)} async-done(((bf16[2048,1536]{1,0:T(8,128)(2,1)}), bf16[512,1536]{1,0:T(8,128)(2,1)}) %reduce-scatter.4.cloned.1.call-update) | async-done | bytes 1572880 | tf_op jit(solution)/shard_map/reduce_scatter | solution.py:276
  531.1 7.0 fusion.66
  539.2 39.8 %psum.55 = s32[8]{0:T(128)} all-reduce(s32[8]{0:T(128)} %convert_element_type.151), channel_id=1, replica_groups=mesh['blk'=4,'expert'=8] {'blk','expert'}, use_global_device_ids=true, to_apply=%region_37.38 | all-reduce | flops 8 | bytes 64 | tf_op jit(solution)/shard_map/psum | solution.py:94
  594.8 57.1 %reduce-scatter.8.cloned.1.call-done = bf16[1,768,768]{2,1,0:T(8,128)(2,1)} async-done(((bf16[1,3072,768]{2,1,0:T(8,128)(2,1)}), bf16[1,768,768]{2,1,0:T(8,128)(2,1)}) %reduce-scatter.8.cloned.1.call-update) | async-done | bytes 1179664 | tf_op jit(solution)/shard_map/reduce_scatter | solution.py:212
  658.5 42.6 %all-reduce = (f32[768]{0:T(1024)}, f32[768]{0:T(1024)}, f32[768,16]{0,1:T(8,128)}, f32[8,16]{1,0:T(8,128)}) all-reduce(f32[768]{0:T(1024)} %get-tuple-element.271, f32[768]{0:T(1024)} %get-tuple-element.269, f32[768,16]{0,1:T(8,128)} %fusion.81, f32[8,16]{1,0:T(8,128)} %add_add_fusion.5), channel_id=1, replica_groups=mesh['blk'=4,'expert'=8] {'blk','expert'}, use_global_device_ids=true, to_apply=%region_28.29 | all-reduce | flops 13952 | bytes 111616 | tf_op jit(solution)/shard_map/psum | solution.py:285
  705.6 145.0 %all-reduce.4.cloned.1.call-done = (f32[768,2304]{1,0:T(8,128)}, f32[768,768]{1,0:T(8,128)}) async-done(((f32[768,2304]{1,0:T(8,128)}, f32[768,768]{1,0:T(8,128)}), (f32[768,2304]{1,0:T(8,128)}, f32[768,768]{1,0:T(8,128)})) %all-reduce.4.cloned.1.call-update) | async-done | bytes 9437200 | tf_op jit(solution)/shard_map/psum | solution.py:285
  850.6 6.6 copy.126
  (373 shorter events, 279.3 us)
Async XLA Ops:
  7.2 54.1 %all-gather.5.cloned.1.call-start = ((), (), s32[]{:S(2)}) async-start(), calls=%async_computation.8 | async-start | bytes 3932160 | tf_op jit(solution)/shard_map/all_gather | solution.py:133
  14.4 93.3 %all-gather.3.cloned.1.call-start = ((), (), s32[]{:S(2)}) async-start(), calls=%async_computation.7 | async-start | bytes 3932160 | tf_op jit(solution)/shard_map/all_gather | solution.py:132
  179.0 143.8 %copy-start.37 = (f32[512]{0:T(512)}, f32[512]{0:T(512)S(1)}, u32[]{:S(2)}) copy-start(f32[512]{0:T(512)S(1)} %broadcast_multiply_fusion) | copy-start | bytes 6148
  180.1 142.8 %copy-start.41 = (f32[512]{0:T(512)}, f32[512]{0:T(512)S(1)}, u32[]{:S(2)}) copy-start(f32[512]{0:T(512)S(1)} %fusion.127) | copy-start | bytes 6148
  181.8 26.2 %all-to-all-start = ((bf16[8,64,768]{2,1,0:T(8,128)(2,1)}), bf16[8,64,768]{2,1,0:T(8,128)(2,1)}, u32[]{:S(2)}, u32[]{:S(2)}) async-start(bf16[8,64,768]{2,1,0:T(8,128)(2,1)} %bitcast.302), calls=%async_computation | async-start | bytes 1572864 | tf_op jit(solution)/shard_map/all_to_all | solution.py:160
  222.3 25.2 %all-to-all-start.1 = ((bf16[8,64,768]{2,1,0:T(8,128)(2,1)}), bf16[8,64,768]{2,1,0:T(8,128)(2,1)}, u32[]{:S(2)}, u32[]{:S(2)}) async-start(bf16[8,64,768]{2,1,0:T(8,128)(2,1)} %fusion.76), calls=%async_computation.1 | async-start | bytes 1572864 | tf_op jit(solution)/shard_map/all_to_all | solution.py:169
  247.5 31.4 %copy-start.13 = (f32[8,64,3072]{2,1,0:T(8,128)S(1)}, f32[8,64,3072]{2,1,0:T(8,128)}, u32[]{:S(2)}) copy-start(f32[8,64,3072]{2,1,0:T(8,128)} %copy-done.12) | copy-start | bytes 18874372
  252.2 36.5 %slice-start = ((s8[4718592]{0:T(1024)(128)(4,1)}), s8[4194304]{0:T(1024)(128)(4,1)S(1)}, s32[]{:S(2)}) async-start(s8[4718592]{0:T(1024)(128)(4,1)} %bitcast.291), calls=%async_computation.13 | async-start | bytes 8388608
  278.9 8.2 copy-start.26
  278.9 9.9 %slice-start.1 = ((s8[4718592]{0:T(1024)(128)(4,1)}), s8[524288]{0:T(1024)(128)(4,1)S(1)}, s32[]{:S(2)}) async-start(s8[4718592]{0:T(1024)(128)(4,1)} %bitcast.291), calls=%async_computation.14 | async-start | bytes 1048576
  292.3 25.2 %all-to-all-start.3 = ((bf16[8,64,768]{2,1,0:T(8,128)(2,1)}), bf16[8,64,768]{2,1,0:T(8,128)(2,1)}, u32[]{:S(2)}, u32[]{:S(2)}) async-start(bf16[8,64,768]{2,1,0:T(8,128)(2,1)} %fusion.71), calls=%async_computation.3 | async-start | bytes 1572864 | tf_op jit(solution)/shard_map/all_to_all | solution.py:207
  296.5 234.5 %reduce-scatter.4.cloned.1.call-start = ((), (), s32[]{:S(2)}) async-start(), calls=%async_computation.9 | async-start | bytes 7864320 | tf_op jit(solution)/shard_map/reduce_scatter | solution.py:276
  301.0 21.8 %copy-start.45 = (f32[512]{0:T(512)}, f32[512]{0:T(512)S(1)}, u32[]{:S(2)}) copy-start(f32[512]{0:T(512)S(1)} %multiply_multiply_fusion.7) | copy-start | bytes 6148
  349.0 7.1 copy-start.4
  381.3 7.1 copy-start.4
  413.6 7.1 copy-start.4
  445.9 7.1 copy-start.4
  462.8 129.2 %reduce-scatter.6.cloned.1.call-start = ((), (), s32[]{:S(2)}) async-start(), calls=%async_computation.10 | async-start | bytes 5898240 | tf_op jit(solution)/shard_map/reduce_scatter | solution.py:209
  469.8 182.1 %reduce-scatter.8.cloned.1.call-start = ((), (), s32[]{:S(2)}) async-start(), calls=%async_computation.11 | async-start | bytes 5898240 | tf_op jit(solution)/shard_map/reduce_scatter | solution.py:212
  478.6 372.0 %all-reduce.4.cloned.1.call-start = ((), (), s32[]{:S(2)}) async-start(), calls=%async_computation.12 | async-start | bytes 18874368 | tf_op jit(solution)/shard_map/psum | solution.py:285
  483.4 47.6 %copy-start.30 = (f32[768]{0:T(1024)S(1)}, f32[768]{0:T(1024)}, u32[]{:S(2)}) copy-start(f32[768]{0:T(1024)} %param.26) | copy-start | bytes 9220
  483.4 47.6 %copy-start.32 = (f32[512]{0:T(512)S(1)}, f32[512]{0:T(512)}, u32[]{:S(2)}) copy-start(f32[512]{0:T(512)} %copy-done.31) | copy-start | bytes 6148
  483.4 47.6 %copy-start.35 = (f32[512]{0:T(512)S(1)}, f32[512]{0:T(512)}, u32[]{:S(2)}) copy-start(f32[512]{0:T(512)} %copy-done.34) | copy-start | bytes 6148
  538.0 45.3 %copy-start.38 = (f32[512]{0:T(512)S(1)}, f32[512]{0:T(512)}, u32[]{:S(2)}) copy-start(f32[512]{0:T(512)} %copy-done.37) | copy-start | bytes 6148
  (88 other events, 247.3 us)
Sparse Core Ops, SparseCore 0:
  14.6 46.6 all-gather.4
  63.7 43.9 all-gather.2
  462.9 68.1 reduce-scatter.3
  533.9 58.0 reduce-scatter.5
  594.8 57.0 reduce-scatter.7
  658.3 192.2 all-reduce.3
where the time goes:
time: 871 us; the launch traced here: 866 us
  waiting for transfers between devices  386 us (44%)
  matrix products  198 us (23%)
  blocking collectives  106 us (12%)
  local copies, waits for them, and re-layouts  80.4 us (9%)
  other arithmetic  59.3 us (7%)
  between operations  15 us (2%)
  starting transfers between devices  14.4 us (2%)
    psum x1, waiting for transfers between devices, body(): lax.psum((grad_qkv, grad_proj, grad_attn_gain, grad_moe_gain, grad_route,...  145 us
    reduce_scatter x1, waiting for transfers between devices, body(): lax.psum_scatter(grad_second.astype(jnp.bfloat16), 'blk', scatter_dimensi...  57.1 us
    reduce_scatter x1, waiting for transfers between devices, body(): lax.psum_scatter(all_terms.astype(jnp.bfloat16), 'blk', scatter_dimension...  43.8 us
    all_gather x1, waiting for transfers between devices, body(): lax.all_gather(value_local, 'blk', axis=0, tiled=True)  42.8 us
    psum x1, blocking collectives, body(): lax.psum((grad_qkv, grad_proj, grad_attn_gain, grad_moe_gain, grad_route,...  42.6 us
    all_gather x1, waiting for transfers between devices, body(): lax.all_gather(key_local, 'blk', axis=0, tiled=True)  41.7 us
    psum x1, blocking collectives, body(): total_counts = lax.psum(count_rows.astype(jnp.int32), ('blk', 'expert'))  39.8 us
    dot_general x8, matrix products, masked_scores(): jnp.einsum('qhd,khd->hqk', queries, key_rows, preferred_element_type=jnp....  33.7 us
  transfers between devices with their start and end apart: 9, of which 9 were waited for; matrix products, arithmetic and copies ran while one was open for 8% of the time, Pallas kernels for 0%

commit v1 on v0

--- a/solution.py
+++ b/solution.py
@@ -1,6 +1,10 @@
+import functools
+
 import jax
 import jax.numpy as jnp
 from jax import lax
+from jax.experimental import pallas as pl
+from jax.experimental.pallas import tpu as pltpu
 from jax.sharding import PartitionSpec as P
 
 HEADS = 12
@@ -61,7 +65,7 @@
     return result
 
 
-def body(
+def general_body(
     tokens,
     cotangent,
     loss_mask,
@@ -302,6 +306,737 @@
     )
 
 
+MESH = pl.DeviceIdType.MESH
+F32 = jnp.float32
+BF16 = jnp.bfloat16
+VMEM_BYTES = 58 * 1024 * 1024
+
+
+def dot(left, right, precision=None):
+    return lax.dot_general(
+        left, right, (((1,), (0,)), ((), ())), precision=precision, preferred_element_type=F32
+    )
+
+
+def dot_nt(left, right, precision=None):
+    return lax.dot_general(
+        left, right, (((1,), (1,)), ((), ())), precision=precision, preferred_element_type=F32
+    )
+
+
+def dot_tn(left, right, precision=None):
+    return lax.dot_general(
+        left, right, (((0,), (0,)), ((), ())), precision=precision, preferred_element_type=F32
+    )
+
+
+def rows_at(index, size):
+    return pl.ds(pl.multiple_of(index * size, size), size)
+
+
+def places():
+    blk = lax.axis_index("blk")
+    expert = lax.axis_index("expert")
+    return blk, expert, blk + 1 - 2 * lax.rem(blk, 2), lax.rem(blk + 2, 4), 3 - blk
+
+
+def greet(peers):
+    barrier = pltpu.get_barrier_semaphore()
+    for peer in peers:
+        pl.semaphore_signal(barrier, inc=1, device_id=peer, device_id_type=MESH)
+    return lambda: pl.semaphore_wait(barrier, len(peers))
+
+
+def push(src, dst, sems, index, peer):
+    copy = pltpu.make_async_remote_copy(
+        src_ref=src,
+        dst_ref=dst,
+        send_sem=sems.at[0, index],
+        recv_sem=sems.at[1, index],
+        device_id=peer,
+        device_id_type=MESH,
+    )
+    copy.start()
+    return copy
+
+
+def standardise(values):
+    average = jnp.mean(values, axis=-1, keepdims=True)
+    centered = values - average
+    scale = lax.rsqrt(jnp.mean(centered * centered, axis=-1, keepdims=True) + EPSILON)
+    return centered * scale, scale
+
+
+def lower_triangle(keys, queries):
+    return lax.broadcasted_iota(jnp.int32, (keys, queries), 0) <= lax.broadcasted_iota(
+        jnp.int32, (keys, queries), 1
+    )
+
+
+class BlockGather:
+    def __init__(self, buf, sems, base, rows):
+        self.buf, self.sems, self.base, self.rows = buf, sems, base, rows
+
+    def part(self, blk, half):
+        size = self.rows // 2
+        return self.buf.at[pl.ds(pl.multiple_of(blk * self.rows + half * size, size), size)]
+
+    def send(self, blk, half, index, peer):
+        ref = self.part(blk, half)
+        return push(ref, ref, self.sems, self.base + index, peer)
+
+    def start(self):
+        blk, expert, bx, by, bd = places()
+        self.copies = [
+            self.send(blk, 0, 0, (bx, expert)),
+            self.send(blk, 1, 1, (by, expert)),
+            self.send(blk, 1, 2, (bx, expert)),
+            self.send(blk, 0, 3, (by, expert)),
+        ]
+
+    def forward(self):
+        blk, expert, bx, by, bd = places()
+        self.copies[0].wait_recv()
+        self.copies.append(self.send(bx, 0, 4, (by, expert)))
+        self.copies[1].wait_recv()
+        self.copies.append(self.send(by, 1, 5, (bx, expert)))
+
+    def wait_neighbours(self):
+        self.copies[2].wait_recv()
+        self.copies[3].wait_recv()
+
+    def wait_diagonal(self):
+        self.copies[4].wait_recv()
+        self.copies[5].wait_recv()
+
+    def wait_sends(self):
+        for copy in self.copies:
+            copy.wait_send()
+
+
+class ExpertExchange:
+    def __init__(self, src, dst, sems, base, rows, dst_base):
+        self.src, self.dst, self.sems, self.base, self.rows, self.dst_base = (
+            src, dst, sems, base, rows, dst_base)
+
+    def start(self):
+        blk, expert = lax.axis_index("blk"), lax.axis_index("expert")
+        n = lax.axis_size("expert")
+        self.copies = []
+        place = pl.ds(pl.multiple_of(self.dst_base + expert * self.rows, self.rows), self.rows)
+        for shift in range(1, n):
+            peer = lax.rem(expert + shift, n)
+            self.copies.append(
+                push(self.src.at[rows_at(peer, self.rows)], self.dst.at[place], self.sems,
+                     self.base + shift - 1, (blk, peer))
+            )
+        self.dst[place] = self.src[rows_at(expert, self.rows)]
+
+    def wait(self):
+        for copy in self.copies:
+            copy.wait_recv()
+        for copy in self.copies:
+            copy.wait_send()
+
+
+def blk_peers():
+    blk, expert, bx, by, bd = places()
+    return [(bx, expert), (by, expert), (bd, expert)]
+
+
+def expert_peers():
+    blk, expert = lax.axis_index("blk"), lax.axis_index("expert")
+    n = lax.axis_size("expert")
+    return [(blk, lax.rem(expert + shift, n)) for shift in range(1, n)]
+
+
+def attend_kernel(
+    tok_ref, gain_ref, wqkv_ref, cot_ref, rows_ref, cols_ref,
+    nall_ref, qkv_ref, out_ref, lse_ref, att_ref, target_row_ref, target_col_ref, cot_in_ref,
+    w_s, wt_s, k_s, att_s, cot_s, w_sem, gather_sems, cot_sems, att_sems,
+):
+    blk, expert, bx, by, bd = places()
+    tok = tok_ref.shape[0]
+    width = tok_ref.shape[1]
+    heads = HEADS // 4
+    group = heads * HEAD_DIM
+    arrived = greet(blk_peers() + expert_peers())
+    odd = lax.rem(blk, 2)
+    loads = []
+    for part in range(3):
+        first = pl.multiple_of(part * width + blk * group - odd * 64, 128)
+        loads.append(
+            pltpu.make_async_copy(wqkv_ref.at[:, pl.ds(first, 256)], w_s.at[part], w_sem.at[part])
+        )
+        loads[-1].start()
+    xhat, _ = standardise(tok_ref[...].astype(F32))
+    nall_ref[rows_at(blk, tok), :] = (xhat * gain_ref[...]).astype(BF16)
+    arrived()
+    gather = BlockGather(nall_ref, gather_sems, 0, tok)
+    gather.start()
+
+    capacity = tok // 8
+    route_row, prio_row, mask_row = rows_ref[0:1, :], rows_ref[1:2, :], rows_ref[2:3, :]
+    route_col, prio_col = cols_ref[:, 0:1], cols_ref[:, 1:2]
+    same = route_col == route_row
+    slot_row = jnp.sum(jnp.where(same & (prio_col < prio_row), 1.0, 0.0), axis=0, keepdims=True)
+    slot_col = jnp.sum(jnp.where(same & (prio_row < prio_col), 1.0, 0.0), axis=1, keepdims=True)
+    target_row = jnp.where(slot_row < capacity, route_row * capacity + slot_row, -1.0)
+    target_col = jnp.where(slot_col < capacity, route_col * capacity + slot_col, -1.0)
+    target_row_ref[...] = jnp.broadcast_to(target_row, target_row_ref.shape)
+    target_col_ref[...] = jnp.broadcast_to(target_col, target_col_ref.shape)
+    slots = lax.broadcasted_iota(jnp.int32, (tok, tok), 0).astype(F32)
+    chosen = jnp.where((slots == target_row) & (mask_row > 0.0), 1.0, 0.0).astype(BF16)
+    cot_s[...] = dot(chosen, cot_ref[...]).astype(BF16)
+    cot_move = ExpertExchange(cot_s, cot_in_ref, cot_sems, 0, capacity, 0)
+    cot_move.start()
+
+    for part in range(3):
+        loads[part].wait()
+        wide = w_s[part]
+        narrow = jnp.where(odd == 1, wide[:, 64:256], wide[:, 0:192])
+        wt_s[part * group : (part + 1) * group, :] = narrow.T
+
+    def project(where):
+        cols = rows_at(where, tok)
+        mixed = dot_nt(wt_s[...], nall_ref[cols, :]).astype(BF16)
+        qkv_ref[0:group, cols] = mixed[0:group] * BF16(HEAD_DIM**-0.5)
+        qkv_ref[group:, cols] = mixed[group:]
+        for head in range(heads):
+            k_s[head, cols, :] = mixed[group + head * 64 : group + (head + 1) * 64].T
+
+    project(blk)
+    gather.forward()
+    gather.wait_neighbours()
+    project(bx)
+    project(by)
+    gather.wait_diagonal()
+    project(bd)
+
+    half = tok // 2
+
+    def scores(i, head):
+        q = qkv_ref[head * 64 : (head + 1) * 64, i * tok : (i + 1) * tok]
+        upper = dot(k_s[head, i * tok : i * tok + half, :], q)
+        upper = jnp.where(lower_triangle(half, tok), upper, MASKED)
+        lower = dot(k_s[head, i * tok + half : (i + 1) * tok, :], q[:, half:])
+        lower = jnp.where(lower_triangle(half, half), lower, MASKED)
+        top = jnp.max(upper, axis=0, keepdims=True)
+        low_top = jnp.max(lower, axis=0, keepdims=True)
+        top = jnp.concatenate([top[:, :half], jnp.maximum(top[:, half:], low_top)], axis=1)
+        if i == 0:
+            return top, upper, lower, None
+        past = dot(k_s[head, 0 : i * tok, :], q)
+        return jnp.maximum(top, jnp.max(past, axis=0, keepdims=True)), upper, lower, past
+
+    sends = []
+
+    def finish(i, head, found):
+        top, upper, lower, past = found
+        v = qkv_ref[2 * group + head * 64 : 2 * group + (head + 1) * 64, :]
+        upper = jnp.exp(upper - top)
+        lower = jnp.exp(lower - top[:, half:])
+        total = jnp.sum(upper, axis=0, keepdims=True)
+        low_total = jnp.sum(lower, axis=0, keepdims=True)
+        total = jnp.concatenate([total[:, :half], total[:, half:] + low_total], axis=1)
+        result = dot(v[:, i * tok : i * tok + half], upper.astype(BF16))
+        low_result = dot(v[:, i * tok + half : (i + 1) * tok], lower.astype(BF16))
+        result = jnp.concatenate([result[:, :half], result[:, half:] + low_result], axis=1)
+        if i:
+            past = jnp.exp(past - top)
+            total = total + jnp.sum(past, axis=0, keepdims=True)
+            result = result + dot(v[:, 0 : i * tok], past.astype(BF16))
+        result = result / total
+        place = slice(head * 64, (head + 1) * 64)
+        out_ref[place, i * tok : (i + 1) * tok] = result
+        lse_ref[head : head + 1, i * tok : (i + 1) * tok] = top + jnp.log(total)
+        att_s[place, i * tok : (i + 1) * tok] = result.astype(BF16)
+        there = pl.ds(pl.multiple_of(blk * group + head * 64, 64), 64)
+
+        def copy():
+            return pltpu.make_async_remote_copy(
+                src_ref=att_s.at[place, i * tok : (i + 1) * tok],
+                dst_ref=att_ref.at[there],
+                send_sem=att_sems.at[0, i * heads + head],
+                recv_sem=att_sems.at[1, blk * heads + head],
+                device_id=(i, expert),
+                device_id_type=MESH,
+            )
+
+        @pl.when(blk != i)
+        def _():
+            copy().start()
+
+        @pl.when(blk == i)
+        def _():
+            att_ref[there, :] = result.astype(BF16)
+
+        sends.append((i, copy))
+
+    before = None
+    for i in range(4):
+        for head in range(heads):
+            found = scores(i, head)
+            if before is not None:
+                finish(*before)
+            before = (i, head, found)
+    finish(*before)
+
+    for i, copy in sends:
+        @pl.when(blk != i)
+        def _():
+            copy().wait_send()
+
+    for source in range(4):
+        @pl.when(blk != source)
+        def _():
+            for head in range(heads):
+                there = pl.ds(source * group + head * 64, 64)
+                pltpu.make_async_remote_copy(
+                    src_ref=att_s.at[0:64, 0:tok],
+                    dst_ref=att_ref.at[there],
+                    send_sem=att_sems.at[0, source * heads + head],
+                    recv_sem=att_sems.at[1, source * heads + head],
+                    device_id=(source, expert),
+                    device_id_type=MESH,
+                ).wait_recv()
+
+    cot_move.wait()
+    gather.wait_sends()
+
+
+def gelu_pair(hidden):
+    squared = hidden * hidden
+    curve = jnp.tanh(0.7978845608028654 * hidden * (1.0 + 0.044715 * squared))
+    half = 0.5 * (1.0 + curve)
+    slope = half + 0.5 * hidden * (1.0 - curve * curve) * (
+        0.7978845608028654 * (1.0 + 0.134145 * squared)
+    )
+    return hidden * half, slope
+
+
+def spread(row, size):
+    shape = (size, row.shape[1])
+    eye = lax.broadcasted_iota(jnp.int32, shape, 0) == lax.broadcasted_iota(jnp.int32, shape, 1)
+    return jnp.sum(jnp.where(eye, row, 0.0), axis=1, keepdims=True)
+
+
+def flatten(column, width):
+    shape = (column.shape[0], width)
+    eye = lax.broadcasted_iota(jnp.int32, shape, 0) == lax.broadcasted_iota(jnp.int32, shape, 1)
+    return jnp.sum(jnp.where(eye, column, 0.0), axis=0, keepdims=True)
+
+
+def expert_kernel(
+    att_ref, tok_ref, proj_ref, gain_ref, route_ref, anchor_ref, cols_ref, target_row_ref,
+    target_col_ref, cot_ref, cot_in_ref, first_ref, second_ref,
+    result_ref, residual_ref, gate_ref, grad_residual_ref, grad_att_ref, grad_proj_ref, small_ref,
+    buf_ref, cots_ref, gates_ref,
+    first_s, second_s, go_s, gate_s, grad_s, back_s, score_s, score_in_s, res_acc, sent_acc, grad_in_s,
+    w_sem, go_sems, gate_sems, back_sems, score_sems, cots_sems, buf_sems, gates_sems,
+):
+    blk, expert, bx, by, bd = places()
+    tok, width = tok_ref.shape
+    experts = 8
+    capacity = tok // experts
+    here = rows_at(blk, tok)
+    arrived = greet(blk_peers() + expert_peers())
+    loads = [
+        pltpu.make_async_copy(first_ref, first_s, w_sem.at[0]),
+        pltpu.make_async_copy(second_ref, second_s, w_sem.at[1]),
+    ]
+    for load in loads:
+        load.start()
+    cots_ref[here, :] = cot_in_ref[...]
+
+    residual = tok_ref[...].astype(F32) + dot_tn(att_ref[...], proj_ref[...])
+    residual_ref[...] = residual
+    xhat, scale = standardise(residual)
+    normed = xhat * gain_ref[...]
+    normed_low = normed.astype(BF16)
+    target_row, target_col = target_row_ref[0:1, :], target_col_ref[:, 0:1]
+    slots = lax.broadcasted_iota(jnp.int32, (tok, tok), 0).astype(F32)
+    go_s[...] = dot(jnp.where(slots == target_row, 1.0, 0.0).astype(BF16), normed_low).astype(BF16)
+    arrived()
+    cots = BlockGather(cots_ref, cots_sems, 0, tok)
+    cots.start()
+    go = ExpertExchange(go_s, buf_ref, go_sems, 0, capacity, blk * tok)
+    go.start()
+
+    route_col = cols_ref[:, 0:1]
+    projected = dot(normed, route_ref[...], TOP_PRECISION)
+    unit_scale = lax.rsqrt(1.0 + jnp.sum(projected * projected, axis=1, keepdims=True))
+    unit = projected * unit_scale
+    anchor = anchor_ref[...]
+    anchor_scale = lax.rsqrt(1.0 + jnp.sum(anchor * anchor, axis=1, keepdims=True))
+    anchor_unit = anchor * anchor_scale
+    logits = dot_nt(unit, anchor_unit, TOP_PRECISION) / ROUTER_SOFTNESS
+    soft = jnp.exp(logits - jnp.max(logits, axis=1, keepdims=True))
+    soft = soft / jnp.sum(soft, axis=1, keepdims=True)
+    onehot = jnp.where(
+        lax.broadcasted_iota(jnp.int32, (tok, experts), 1).astype(F32) == route_col, 1.0, 0.0
+    )
+    gate = jnp.sum(soft * onehot, axis=1, keepdims=True)
+    gate_ref[...] = jnp.broadcast_to(gate, gate_ref.shape)
+    lane = lax.broadcasted_iota(jnp.int32, (tok, 128), 1).astype(F32)
+    lane = jnp.where(lane < capacity, lane, 1e6)
+    for peer in range(experts):
+        row = jnp.sum(
+            jnp.where(target_col == peer * capacity + lane, gate, 0.0), axis=0, keepdims=True
+        )
+        gate_s[peer * 8 : (peer + 1) * 8, :] = jnp.broadcast_to(row, (8, 128))
+    gates = ExpertExchange(gate_s, gates_ref, gate_sems, 0, 8, blk * 64)
+    gates.start()
+
+    cots.forward()
+    go.wait()
+    gates.wait()
+    buf = BlockGather(buf_ref, buf_sems, 0, tok)
+    buf.start()
+    gates_here = gates_ref.at[rows_at(blk, 64)]
+    gates_out = [
+        push(gates_here, gates_here, gates_sems, n, peer) for n, peer in enumerate(blk_peers())
+    ]
+    cots.wait_neighbours()
+    cots.wait_diagonal()
+    buf.forward()
+
+    for source in range(experts):
+        chunk = slice(source * capacity, (source + 1) * capacity)
+        rate = spread(gates_ref[pl.ds(blk * 64 + source * 8, 8), :][0:1, :], capacity)
+        grad_in_s[chunk, :] = (cot_in_ref[chunk, :].astype(F32) * rate).astype(BF16)
+    for load in loads:
+        load.wait()
+    tile = 768
+    x = buf_ref[here, :]
+    grad_in = grad_in_s[...]
+    for t in range(first_s.shape[1] // tile):
+        cut = slice(t * tile, (t + 1) * tile)
+        hidden = dot(x, first_s[:, cut])
+        act, slope = gelu_pair(hidden)
+        part = dot(act.astype(BF16), second_s[cut, :])
+        grad_hidden = (dot_nt(grad_in, second_s[cut, :]) * slope).astype(BF16)
+        sent = dot_nt(grad_hidden, first_s[:, cut])
+        if t == 0:
+            res_acc[...] = part
+            sent_acc[...] = sent
+        else:
+            res_acc[...] += part
+            sent_acc[...] += sent
+    grad_s[...] = sent_acc[...].astype(BF16)
+    back = ExpertExchange(grad_s, back_s, back_sems, 0, capacity, 0)
+    back.start()
+    result = res_acc[...].astype(BF16)
+    result_ref[...] = result
+    score = jnp.sum(result.astype(F32) * cot_in_ref[...].astype(F32), axis=1, keepdims=True)
+    for source in range(experts):
+        row = flatten(score[source * capacity : (source + 1) * capacity], 128)
+        score_s[source * 8 : (source + 1) * 8, :] = jnp.broadcast_to(row, (8, 128))
+    scores = ExpertExchange(score_s, score_in_s, score_sems, 0, 8, 0)
+    scores.start()
+    grad_out = cot_ref[...].astype(F32) * cols_ref[:, 2:3]
+
+    scores.wait()
+    grad_gate = jnp.zeros((tok, 1), F32)
+    for peer in range(experts):
+        row = score_in_s[peer * 8 : peer * 8 + 1, :]
+        grad_gate += jnp.sum(
+            jnp.where(target_col == peer * capacity + lane, row, 0.0), axis=1, keepdims=True
+        )
+    grad_logits = grad_gate * gate * (onehot - soft) / ROUTER_SOFTNESS
+    grad_unit = dot(grad_logits, anchor_unit, TOP_PRECISION)
+    grad_projected = unit_scale * (
+        grad_unit - unit * jnp.sum(unit * grad_unit, axis=1, keepdims=True)
+    )
+    grad_anchor_unit = dot_tn(grad_logits, unit, TOP_PRECISION)
+    grad_anchor = anchor_scale * (
+        grad_anchor_unit
+        - anchor_unit * jnp.sum(anchor_unit * grad_anchor_unit, axis=1, keepdims=True)
+    )
+    rdim = route_ref.shape[1]
+    small_ref[...] = jnp.zeros_like(small_ref)
+    small_ref[0:rdim, :] = dot_tn(grad_projected, normed, TOP_PRECISION)
+    small_ref[rdim : rdim + experts, 0:rdim] = grad_anchor
+    counts = jnp.sum(onehot, axis=0, keepdims=True)
+    small_ref[rdim + experts + 2 : rdim + experts + 3, 0:experts] = counts
+    router_rows = dot_nt(grad_projected, route_ref[...], TOP_PRECISION)
+
+    back.wait()
+    lanes = lax.broadcasted_iota(jnp.int32, (tok, tok), 1).astype(F32)
+    moe_rows = dot(jnp.where(lanes == target_col, 1.0, 0.0).astype(BF16), back_s[...])
+    grad_normed = moe_rows + router_rows
+    small_ref[rdim + experts : rdim + experts + 1, :] = jnp.sum(
+        grad_normed * xhat, axis=0, keepdims=True
+    )
+    grad_xhat = grad_normed * gain_ref[...]
+    grad_residual = grad_out + scale * (
+        grad_xhat
+        - jnp.mean(grad_xhat, axis=1, keepdims=True)
+        - xhat * jnp.mean(grad_xhat * xhat, axis=1, keepdims=True)
+    )
+    grad_residual_ref[...] = grad_residual
+    grad_low = grad_residual.astype(BF16)
+    grad_att_ref[...] = dot_nt(proj_ref[...], grad_low).astype(BF16)
+    grad_proj_ref[...] = dot(att_ref[...], grad_low)
+
+    buf.wait_neighbours()
+    buf.wait_diagonal()
+    cots.wait_sends()
+    buf.wait_sends()
+    for copy in gates_out:
+        copy.wait()
+
+
+def expert_weights_kernel(
+    buf_ref, cots_ref, gates_ref, first_ref, second_ref, grad_first_ref, grad_second_ref,
+    first_t, acc,
+):
+    slots, width = buf_ref.shape
+    first_t[...] = first_ref[...].T
+    step = 512
+    for t in range(slots // step):
+        cut = slice(t * step, (t + 1) * step)
+        rates = [spread(gates_ref[t * 64 + s * 8 : t * 64 + s * 8 + 1, :], 64) for s in range(8)]
+        rate = jnp.concatenate(rates, axis=0)
+        x = buf_ref[cut, :]
+        grad_in = (cots_ref[cut, :].astype(F32) * rate).astype(BF16)
+        act, slope = gelu_pair(dot_nt(first_t[...], x))
+        grad_hidden = (dot_nt(second_ref[...], grad_in) * slope).astype(BF16)
+        grad_second = dot(act.astype(BF16), grad_in)
+        grad_first = dot(grad_hidden, x)
+        if t == 0:
+            grad_second_ref[...] = grad_second
+            acc[...] = grad_first
+        else:
+            grad_second_ref[...] += grad_second
+            acc[...] += grad_first
+    grad_first_ref[...] = acc[...].T
+
+
+def attend_back_kernel(
+    grad_att_ref, qkv_ref, out_ref, lse_ref, nall_ref, result_ref, residual_ref, gate_ref,
+    target_col_ref, gain_ref, wqkv_ref,
+    block_out_ref, dqkv_home_ref, grad_group_ref, attn_gain_ref,
+    do_t, dq_s, dqkv_s, q_s, k_s, v_s, do_s, back_s, w_s, wt_s,
+    w_sem, att_sems, back_sems, home_sems,
+):
+    blk, expert, bx, by, bd = places()
+    tok = grad_att_ref.shape[1]
+    width = grad_att_ref.shape[0]
+    heads = HEADS // 4
+    group = heads * HEAD_DIM
+    here = rows_at(blk, tok)
+    length = qkv_ref.shape[1]
+    arrived = greet(blk_peers() + expert_peers())
+    odd = lax.rem(blk, 2)
+    loads = []
+    for part in range(3):
+        first = pl.multiple_of(part * width + blk * group - odd * 64, 128)
+        loads.append(
+            pltpu.make_async_copy(wqkv_ref.at[:, pl.ds(first, 256)], w_s.at[part], w_sem.at[part])
+        )
+        loads[-1].start()
+    arrived()
+    mine = rows_at(blk, group)
+    att_copies = [
+        push(grad_att_ref.at[rows_at(peer[0], group)], do_t.at[:, here], att_sems, n, peer)
+        for n, peer in enumerate(blk_peers())
+    ]
+    back = ExpertExchange(result_ref, back_s, back_sems, 0, tok // 8, 0)
+    back.start()
+    do_t[:, here] = grad_att_ref[mine, :]
+    for head in range(heads):
+        cut = slice(head * 64, (head + 1) * 64)
+        q_s[head] = qkv_ref[cut, :].T
+        k_s[head] = qkv_ref[group + head * 64 : group + (head + 1) * 64, :].T
+        v_s[head] = qkv_ref[2 * group + head * 64 : 2 * group + (head + 1) * 64, :].T
+    for part in range(3):
+        loads[part].wait()
+        wide = w_s[part]
+        narrow = jnp.where(odd == 1, wide[:, 64:256], wide[:, 0:192])
+        wt_s[part * group : (part + 1) * group, :] = narrow.T
+    for copy in att_copies:
+        copy.wait_recv()
+    for head in range(heads):
+        do_s[head] = do_t[head * 64 : (head + 1) * 64, :].T
+
+    home = []
+    for head in range(heads):
+        cut = slice(head * 64, (head + 1) * 64)
+        kt_cut = slice(group + head * 64, group + (head + 1) * 64)
+        vt_cut = slice(2 * group + head * 64, 2 * group + (head + 1) * 64)
+        delta = jnp.sum(out_ref[cut, :] * do_t[cut, :].astype(F32), axis=0, keepdims=True)
+        for j in range(4):
+            keys = slice(j * tok, (j + 1) * tok)
+            queries = slice(j * tok, length)
+            s = dot(k_s[head, keys, :], qkv_ref[cut, queries])
+            p = jnp.exp(s - lse_ref[head : head + 1, queries])
+            allowed = lower_triangle(tok, length - j * tok)
+            p = jnp.where(allowed, p, 0.0)
+            dp = dot(v_s[head, keys, :], do_t[cut, queries])
+            ds = (p * (dp - delta[:, queries])).astype(BF16)
+            dv = dot(p.astype(BF16), do_s[head, queries, :])
+            dk = dot(ds, q_s[head, queries, :])
+            dqkv_s[kt_cut, keys] = dk.T.astype(BF16)
+            dqkv_s[vt_cut, keys] = dv.T.astype(BF16)
+            dq = dot(qkv_ref[kt_cut, keys], ds)
+            if j == 0:
+                dq_s[...] = dq
+            else:
+                dq_s[:, queries] += dq
+        dqkv_s[cut, :] = (dq_s[...] * HEAD_DIM**-0.5).astype(BF16)
+        for n, peer in enumerate(blk_peers()):
+            for part in range(3):
+                src = dqkv_s.at[part * group + head * 64 : part * group + (head + 1) * 64,
+                                rows_at(peer[0], tok)]
+                there = pl.ds(pl.multiple_of(part * width + blk * group + head * 64, 64), 64)
+                home.append(
+                    push(src, dqkv_home_ref.at[there], home_sems, (n * heads + head) * 3 + part, peer)
+                )
+        for part in range(3):
+            there = pl.ds(pl.multiple_of(part * width + blk * group + head * 64, 64), 64)
+            dqkv_home_ref[there, :] = dqkv_s[
+                part * group + head * 64 : part * group + (head + 1) * 64, here]
+
+    grad_group = dot(dqkv_s[...], nall_ref[...])
+    grad_group_ref[...] = grad_group
+    attn_gain = jnp.sum(grad_group * wt_s[...].astype(F32), axis=0, keepdims=True) / gain_ref[...]
+    attn_gain_ref[...] = jnp.broadcast_to(attn_gain, attn_gain_ref.shape)
+
+    back.wait()
+    lanes = lax.broadcasted_iota(jnp.int32, (tok, tok), 1).astype(F32)
+    chosen = jnp.where(lanes == target_col_ref[:, 0:1], 1.0, 0.0).astype(BF16)
+    fetched = dot(chosen, back_s[...])
+    block_out_ref[...] = (residual_ref[...] + gate_ref[:, 0:1] * fetched).astype(BF16)
+    for copy in att_copies:
+        copy.wait_send()
+    for copy in home:
+        copy.wait_send()
+    for copy in home:
+        copy.wait_recv()
+
+
+def tokens_kernel(dqkv_ref, wqkv_ref, tok_ref, gain_ref, grad_residual_ref, out_ref):
+    xhat, scale = standardise(tok_ref[...].astype(F32))
+    grad_normed = dot(wqkv_ref[...], dqkv_ref[...]).T
+    grad_xhat = grad_normed * gain_ref[...]
+    out_ref[...] = grad_residual_ref[...] + scale * (
+        grad_xhat
+        - jnp.mean(grad_xhat, axis=1, keepdims=True)
+        - xhat * jnp.mean(grad_xhat * xhat, axis=1, keepdims=True)
+    )
+
+
+def call(kernel, name, args, outs, scratch, in_any=(), collective=None):
+    specs = [
+        pl.BlockSpec(memory_space=pl.ANY if n in in_any else pltpu.VMEM) for n in range(len(args))
+    ]
+    shapes = tuple(jax.ShapeDtypeStruct(shape, dtype) for shape, dtype in outs)
+    return pl.pallas_call(
+        kernel,
+        out_shape=shapes,
+        in_specs=specs,
+        out_specs=tuple(pl.BlockSpec(memory_space=pltpu.VMEM) for _ in outs),
+        scratch_shapes=scratch,
+        name=name,
+        compiler_params=pltpu.CompilerParams(
+            vmem_limit_bytes=VMEM_BYTES,
+            collective_id=collective,
+            has_side_effects=collective is not None,
+        ),
+    )(*args)
+
+
+def fast_body(
+    tokens, cotangent, loss_mask, routes, priority, histogram, qkv_weight, proj_weight, attn_gain,
+    moe_gain, route_weight, anchor_table, first_weight, second_weight,
+):
+    tok, width = tokens.shape[1:]
+    blocks, experts = lax.axis_size("blk"), lax.axis_size("expert")
+    length = tok * blocks
+    heads = HEADS // blocks
+    group = heads * HEAD_DIM
+    hidden = first_weight.shape[2]
+    x, cot = tokens[0], cotangent[0]
+    rows = jnp.stack([routes[0, :, 0], priority[0, 0], loss_mask[0]]).astype(F32)
+    rows = jnp.pad(rows, ((0, 5), (0, 0)))
+    cols = rows.T
+    gain1, gain2 = attn_gain[None], moe_gain[None]
+    dma = pltpu.SemaphoreType.DMA
+    nall, qkv, out, lse, att, target_row, target_col, cot_in = call(
+        attend_kernel, "attend", (x, gain1, qkv_weight, cot, rows, cols),
+        [((length, width), BF16), ((3 * group, length), BF16), ((group, length), F32),
+         ((8, length), F32), ((width, tok), BF16), ((8, tok), F32), ((tok, 128), F32),
+         ((tok, width), BF16)],
+        [pltpu.VMEM((3, width, 256), BF16), pltpu.VMEM((3 * group, width), BF16),
+         pltpu.VMEM((heads, length, HEAD_DIM), BF16), pltpu.VMEM((group, length), BF16),
+         pltpu.VMEM((tok, width), BF16), dma((3,)), dma((2, 6)), dma((2, experts)),
+         dma((2, blocks * heads))],
+        in_any=(2,), collective=1,
+    )
+    (result, residual, gate, grad_residual, grad_att, grad_proj, small, buf, cots, gates) = call(
+        expert_kernel, "expert",
+        (att, x, proj_weight, gain2, route_weight, anchor_table, cols, target_row, target_col, cot,
+         cot_in, first_weight[0], second_weight[0]),
+        [((tok, width), BF16), ((tok, width), F32), ((tok, 128), F32), ((tok, width), F32),
+         ((width, tok), BF16), ((width, width), F32), ((32, width), F32),
+         ((length, width), BF16), ((length, width), BF16), ((blocks * 64, 128), F32)],
+        [pltpu.VMEM((width, hidden), BF16), pltpu.VMEM((hidden, width), BF16),
+         pltpu.VMEM((tok, width), BF16), pltpu.VMEM((64, 128), F32), pltpu.VMEM((tok, width), BF16),
+         pltpu.VMEM((tok, width), BF16), pltpu.VMEM((64, 128), F32), pltpu.VMEM((64, 128), F32),
+         pltpu.VMEM((tok, width), F32), pltpu.VMEM((tok, width), F32), pltpu.VMEM((tok, width), BF16),
+         dma((2,)), dma((2, experts)), dma((2, experts)), dma((2, experts)), dma((2, experts)),
+         dma((2, 6)), dma((2, 6)), dma((2, 3))],
+        in_any=(11, 12), collective=2,
+    )
+    place = lax.axis_index("blk")
+    quarter = hidden // blocks
+    first_part = lax.dynamic_slice_in_dim(first_weight[0], place * quarter, quarter, 1)
+    second_part = lax.dynamic_slice_in_dim(second_weight[0], place * quarter, quarter, 0)
+    grad_first, grad_second = call(
+        expert_weights_kernel, "expert_weights", (buf, cots, gates, first_part, second_part),
+        [((width, quarter), F32), ((quarter, width), F32)],
+        [pltpu.VMEM((quarter, width), BF16), pltpu.VMEM((quarter, width), F32)],
+    )
+    block_out, dqkv, grad_group, attn_row = call(
+        attend_back_kernel, "attend_back",
+        (grad_att, qkv, out, lse, nall, result, residual, gate, target_col, gain1, qkv_weight),
+        [((tok, width), BF16), ((3 * width, tok), BF16), ((3 * group, width), F32), ((8, width), F32)],
+        [pltpu.VMEM((group, length), BF16), pltpu.VMEM((HEAD_DIM, length), F32),
+         pltpu.VMEM((3 * group, length), BF16)]
+        + [pltpu.VMEM((heads, length, HEAD_DIM), BF16)] * 4
+        + [pltpu.VMEM((tok, width), BF16), pltpu.VMEM((3, width, 256), BF16),
+           pltpu.VMEM((3 * group, width), BF16),
+           dma((3,)), dma((2, 3)), dma((2, experts)), dma((2, 27))],
+        in_any=(10,), collective=3,
+    )
+    (grad_tokens,) = call(
+        tokens_kernel, "tokens", (dqkv, qkv_weight, x, gain1, grad_residual),
+        [((tok, width), F32)], [],
+    )
+    small = small.at[route_weight.shape[1] + experts + 1].set(attn_row[0])
+    small = lax.psum(small, ("blk", "expert"))
+    grad_proj = lax.psum(grad_proj.astype(BF16), ("blk", "expert")).astype(F32)
+    grad_group = lax.psum(grad_group.astype(BF16), "expert")
+    gathered = lax.all_gather(grad_group, "blk", axis=0)
+    grad_qkv = gathered.reshape(blocks, 3, group, width).transpose(3, 1, 0, 2)
+    grad_qkv = grad_qkv.reshape(width, 3 * width).astype(F32)
+    rdim = route_weight.shape[1]
+    return (
+        block_out[None],
+        grad_tokens[None],
+        grad_qkv,
+        grad_proj,
+        small[rdim + experts + 1],
+        small[rdim + experts],
+        small[:rdim].T,
+        small[rdim : rdim + experts, :rdim],
+        grad_first[None],
+        grad_second[None],
+        histogram + small[rdim + experts + 2, :experts].astype(jnp.int32),
+    )
+
+
 def solution(mesh):
     in_specs = (
         P("expert", "blk", None),
@@ -332,4 +1067,6 @@
         P("expert", "blk", None),
         P(),
     )
+    blocks, experts = mesh.shape["blk"], mesh.shape["expert"]
+    body = fast_body if (blocks, experts) == (4, 8) else general_body
     return jax.shard_map(body, mesh=mesh, in_specs=in_specs, out_specs=out_specs, check_vma=False)

time: 871 us -> 611 us (0.70)
  Pallas kernels: 0 us -> 219 us
  matrix products: 198 us -> 0 us
  blocking collectives: 106 us -> 0 us
  waiting for transfers between devices: 386 us -> 330 us
  local copies, waits for them, and re-layouts: 80.4 us -> 27.5 us
  other arithmetic: 59.3 us -> 11.2 us
  starting transfers between devices: 14.4 us -> 0.34 us
    pallas_call x0 -> x5, Pallas kernels: none -> 219 us  [call(): pl.pallas_call(kernel, out_shape=shapes, in_specs=specs, out_specs=tuple(...]
    dot_general x50 -> x0, matrix products: 198 us -> none  [the longest x8 33.7 us: masked_scores(): jnp.einsum('qhd,khd->hqk', queries, key_rows, preferred_element_type=jnp....]
    psum x1 -> x3, waiting for transfers between devices: 145 us -> 285 us  [the longest x1 134 us: fast_body(): grad_proj = lax.psum(grad_proj.astype(BF16), ('blk', 'expert')).astype(F32)]
    reduce_scatter x3 -> x0, waiting for transfers between devices: 106 us -> none  [the longest x1 57.1 us: body(): lax.psum_scatter(grad_second.astype(jnp.bfloat16), 'blk', scatter_dimensi...]
    psum x2 -> x0, blocking collectives: 82.4 us -> none  [the longest x1 42.6 us: body(): lax.psum((grad_qkv, grad_proj, grad_attn_gain, grad_moe_gain, grad_route,...]
    all_to_all x3 -> x0, waiting for transfers between devices: 50 us -> none  [the longest x1 19.7 us: body(): lax.all_to_all(outgoing, 'expert', split_axis=0, concat_axis=0, tiled=True)]
    all_gather x2 -> x1, waiting for transfers between devices: 84.5 us -> 45.1 us  [fast_body(): gathered = lax.all_gather(grad_group, 'blk', axis=0)]
    reduce_sum x14 -> x0, other arithmetic: 25.4 us -> none  [the longest x4 14 us: forward_step(): running_sum = running_sum * factor + jnp.sum(weights, axis=2)]
  transfers between devices with their start and end apart: 9 -> 4, of which waited for: 9 -> 4; matrix products, arithmetic and copies ran while one was open for 8% -> 2% of each run, Pallas kernels for 0% -> 4%
where the time goes in v1:
time: 611 us; the launch traced here: 602 us
  waiting for transfers between devices  330 us (54%)
  Pallas kernels  219 us (36%)
  local copies, waits for them, and re-layouts  27.5 us (5%)
  between operations  14.1 us (2%)
  other arithmetic  11.2 us (2%)
    pallas_call x5, Pallas kernels, call(): pl.pallas_call(kernel, out_shape=shapes, in_specs=specs, out_specs=tuple(...  219 us
    psum x1, waiting for transfers between devices, fast_body(): grad_proj = lax.psum(grad_proj.astype(BF16), ('blk', 'expert')).astype(F32)  134 us
    psum x1, waiting for transfers between devices, fast_body(): small = lax.psum(small, ('blk', 'expert'))  98.1 us
    psum x1, waiting for transfers between devices, fast_body(): grad_group = lax.psum(grad_group.astype(BF16), 'expert')  53.3 us
    all_gather x1, waiting for transfers between devices, fast_body(): gathered = lax.all_gather(grad_group, 'blk', axis=0)  45.1 us
  transfers between devices with their start and end apart: 4, of which 4 were waited for; matrix products, arithmetic and copies ran while one was open for 2% of the time, Pallas kernels for 4%

profile of v1, /device:TPU:0, one launch (start us, length us, event | category | flops | bytes accessed | tf_op | source)
XLA Modules:
  0.0 601.8 jit_solution(392633513476054982)
XLA Ops:
  9.0 1.3 broadcast_in_dim.18.gain_ref
  10.2 1.3 broadcast_in_dim.19.gain_ref
  11.5 1.7 copy.47.route_ref
  13.8 52.1 %attend.1 = (bf16[2048,768]{1,0:T(8,128)(2,1)}, bf16[576,2048]{1,0:T(8,128)(2,1)}, f32[192,2048]{1,0:T(8,128)}, f32[8,2048]{1,0:T(8,128)}, bf16[768,512]{1,0:T(8...) custom-call(bf16[512,768]{1,0:T(8,128)(2,1)} %bitcast.32, ...), custom_call_target="tpu_custom_call" | custom-call | tf_op jit(solution)/shard_map/attend/pallas_call | solution.py:935
  66.0 86.9 %expert.1 = (bf16[512,768]{1,0:T(8,128)(2,1)}, f32[512,768]{1,0:T(8,128)}, f32[512,128]{1,0:T(8,128)}, f32[512,768]{1,0:T(8,128)}, bf16[768,512]{1,0:T(8,128)(2,...) custom-call(bf16[768,512]{1,0:T(8,128)(2,1)} %get-tuple-element.47.a, ...), custom_call_target="tpu_custom_call" | custom-call | tf_op jit(solution)/shard_map/expert/pallas_call | solution.py:935
  152.8 54.1 %attend_back.1 = (bf16[512,768]{1,0:T(8,128)(2,1)}, bf16[2304,512]{1,0:T(8,128)(2,1)}, f32[576,768]{1,0:T(8,128)}, f32[8,768]{1,0:T(8,128)}) custom-call(bf16[768,512]{1,0:T(8,128)(2,1)} %get-tuple-element.51.grad_att_ref, bf16[576,2048]{1,0:T(8,128)(2,1)} %get-tuple-element.52.qkv_ref, f32[192,2048]{1,0:T(8,128)} %get-tuple-element.53.out_ref, ...), custom_call_target="tpu_custom_call" | custom-call | tf_op jit(solution)/shard_map/attend_back/pallas_call | solution.py:935
  207.0 2.6 convert_bitcast_fusion.1
  210.4 1.4 scatter.4
  211.9 1.1 convert_element_type.38
  213.2 53.3 %all-reduce.5.cloned.1.call-done = bf16[1,576,768]{2,1,0:T(8,128)(2,1)} async-done(((bf16[1,576,768]{2,1,0:T(8,128)(2,1)}), bf16[1,576,768]{2,1,0:T(8,128)(2,1)}) %all-reduce.5.cloned.1.call-update) | async-done | bytes 884752 | tf_op jit(solution)/shard_map/psum | solution.py:1020
  266.5 7.5 %tokens.1 = f32[512,768]{1,0:T(8,128)} custom-call(bf16[2304,512]{1,0:T(8,128)(2,1)} %get-tuple-element.60.dqkv_ref, bf16[768,2304]{1,0:T(8,128)(2,1)} %wqkv_ref.5, bf16[512,768]{1,0:T(8,128)(2,1)} %bitcast.34, f32[1,768]{1,0:T(1,128)} %broadcast_in_dim.18.gain_ref, f32[512,768]{1,0:T(8,128)} %get-tuple-element.61.grad_residual_ref), custom_call_target="tpu_custom_call" | custom-call | tf_op jit(solution)/shard_map/tokens/pallas_call | solution.py:935
  274.0 3.2 dynamic-slice_bitcast_fusion
  277.2 18.1 %expert_weights.1 = (f32[768,768]{1,0:T(8,128)}, f32[768,768]{1,0:T(8,128)}) custom-call(bf16[2048,768]{1,0:T(8,128)(2,1)} %get-tuple-element.66.buf_ref, bf16[2048,768]{1,0:T(8,128)(2,1)} %get-tuple-element.67.cots_ref, f32[256,128]{1,0:T(8,128)} %get-tuple-element.68.gates_ref, bf16[768,768]{1,0:T(8,128)(2,1)} %get-tuple-element.118.first_ref, ...), custom_call_target="tpu_custom_call" | custom-call | tf_op jit(solution)/shard_map/expert_weights/pallas_call | solution.py:935
  295.3 98.1 %all-reduce.9.cloned.1.call-done = f32[32,768]{1,0:T(8,128)} async-done(((f32[32,768]{1,0:T(8,128)}), f32[32,768]{1,0:T(8,128)}) %all-reduce.9.cloned.1.call-update) | async-done | bytes 98320 | tf_op jit(solution)/shard_map/psum | solution.py:1018
  393.3 1.3 slice.42
  394.6 1.4 slice_reduce_fusion
  396.0 1.2 fusion.1
  397.2 1.4 slice_bitcast_fusion
  398.7 133.5 %all-reduce.7.cloned.1.call-done = bf16[768,768]{1,0:T(8,128)(2,1)} async-done(((bf16[768,768]{1,0:T(8,128)(2,1)}), bf16[768,768]{1,0:T(8,128)(2,1)}) %all-reduce.7.cloned.1.call-update) | async-done | bytes 1179664 | tf_op jit(solution)/shard_map/psum | solution.py:1019
  532.2 2.8 convert_element_type.39
  535.0 45.1 %all-gather.2.cloned.1.call-done = bf16[4,576,768]{2,1,0:T(8,128)(2,1)} async-done(((bf16[1,576,768]{2,1,0:T(8,128)(2,1)}), bf16[4,576,768]{2,1,0:T(8,128)(2,1)}) %all-gather.2.cloned.1.call-update) | async-done | bytes 3538960 | tf_op jit(solution)/shard_map/all_gather | solution.py:1021
  580.1 2.7 convert_bitcast_fusion
  582.8 3.3 copy.48
  586.1 8.0 %copy.49 = f32[768,2304]{1,0:T(8,128)} copy(f32[768,2304]{0,1:T(8,128)} %bitcast.29) | data formatting | bytes 14155776
  (21 shorter events, 4.4 us)
Async XLA Ops:
  7.2 259.3 %all-reduce.5.cloned.1.call-start = ((), (), s32[]{:S(2)}) async-start(), calls=%async_computation | async-start | bytes 1769472 | tf_op jit(solution)/shard_map/psum | solution.py:1020
  207.0 4.9 copy-start
  209.6 183.7 %all-reduce.9.cloned.1.call-start = ((), (), s32[]{:S(2)}) async-start(), calls=%async_computation.3 | async-start | bytes 196608 | tf_op jit(solution)/shard_map/psum | solution.py:1018
  211.8 320.4 %all-reduce.7.cloned.1.call-start = ((), (), s32[]{:S(2)}) async-start(), calls=%async_computation.2 | async-start | bytes 2359296 | tf_op jit(solution)/shard_map/psum | solution.py:1019
  213.0 367.1 %all-gather.2.cloned.1.call-start = ((), (), s32[]{:S(2)}) async-start(), calls=%async_computation.1 | async-start | bytes 4423680 | tf_op jit(solution)/shard_map/all_gather | solution.py:1021
  277.2 118.9 %copy-start.2 = (s32[8]{0:T(128)S(1)}, s32[8]{0:T(128)}, u32[]{:S(2)}) copy-start(s32[8]{0:T(128)} %param.21) | copy-start | bytes 100
  586.1 8.0 %copy-start.1 = (bf16[512,768]{1,0:T(8,128)(2,1)S(1)}, bf16[512,768]{1,0:T(8,128)(2,1)}, u32[]{:S(2)}) copy-start(bf16[512,768]{1,0:T(8,128)(2,1)} %get-tuple-element.59) | copy-start | bytes 2359300
Sparse Core Ops, SparseCore 0:
  209.7 56.7 all-reduce.4
  273.0 120.3 all-reduce.8
  400.2 131.9 all-reduce.6
  533.9 46.1 all-gather.1
